TPU v7x, 32 devices: a whole 2x2x4 slice. The times are simulated.
32 devices in a mesh: groups: 2 (over x), rows: 16 (over z, y, core).
Axes of the slice: x: 2, y: 2, z: 4, core: 2. Of those that a mesh axis runs over, the one named last changes fastest.
Arguments:
- a_blocks: bfloat16 [256, 8, 256, 256], P(('groups', 'rows')), parts along dimension 0, may hold values from -8 to 8
- basis_in: bfloat16 [65536, 128], P(('groups', 'rows')), parts along dimension 0, may hold values from -5 to 5
- pattern: int32 [256, 8], P(('groups', 'rows')), parts along dimension 0, may hold values from 0 to 127, as said below
Outputs:
- basis_out: float32 [65536, 128], P(('groups', 'rows')), parts along dimension 0
- factor: float32 [256, 128], P('groups'), parts along dimension 0
There are 2 independent parts, one for each index of `groups`. A program takes and returns all parts, laid end to end along the dimension named above; each array names one. Nothing has to cross between parts.
Inputs may be any that keep to these rules, and one draw needn't show every extreme that they name: `pattern`: the 64 entries of the block rows of one device name blocks of at most 15 other devices; those naming blocks of any one other device number at most 5 and name at most 1 distinct blocks; all three bounds are reached in every draw. The entries of one block row that name blocks of other devices are distinct.
All inputs are finite; a program needn't handle non-finite values.
Results may differ from a plain program's by a relative error of at most 0.0003.
Values may be sent and summed in bfloat16 or wider, within the bound.
A program may use at most 128 MiB of HBM per device.

v0:
```python
import jax
import jax.numpy as jnp
from jax import lax
from jax.sharding import PartitionSpec as P


def upper_factor_of(matrix):
    return jnp.linalg.cholesky(matrix).T


def shards(a_blocks, basis_in, pattern):
    rank_count = lax.axis_size("rows")
    my_index = lax.axis_index("rows")
    block_rows, slot_count, block_size, unused = a_blocks.shape
    columns = basis_in.shape[1]
    own_blocks = basis_in.reshape(block_rows, block_size, columns)
    ref_count = block_rows * slot_count
    my_cols = pattern.reshape(ref_count)
    my_owner = my_cols // block_rows
    my_local = my_cols - my_owner * block_rows
    remote = my_owner != my_index
    every = lax.all_gather(pattern, "rows", axis=0, tiled=True).reshape(rank_count, ref_count)
    their_owner = every // block_rows
    their_local = every - their_owner * block_rows
    readers = jnp.arange(rank_count, dtype=jnp.int32)
    block_ids = jnp.arange(block_rows, dtype=jnp.int32)
    wanted = (their_owner == my_index) & (readers[:, None] != my_index)
    owners_hot = (my_owner[:, None] == readers[None, :]) & remote[:, None]
    owner_slots = min(ref_count - 1, rank_count - 1)
    slot_depth = (ref_count + owner_slots - 1) // owner_slots
    wanted_int = wanted.astype(jnp.int32)
    rank_in = jnp.cumsum(wanted_int, axis=1) - wanted_int
    by_slot = wanted[:, :, None] & (
        rank_in[:, :, None] == jnp.arange(slot_depth, dtype=jnp.int32)[None, None, :]
    )
    by_block = their_local[:, :, None] == block_ids[None, None, :]
    selection = jnp.einsum(
        "erk,erb->ekb",
        by_slot.astype(jnp.bfloat16),
        by_block.astype(jnp.bfloat16),
        preferred_element_type=jnp.float32,
    ).astype(jnp.bfloat16)
    outgoing = jnp.einsum(
        "ekb,bij->ekij", selection, own_blocks, preferred_element_type=jnp.float32
    ).astype(jnp.bfloat16)
    incoming = lax.all_to_all(outgoing, "rows", split_axis=0, concat_axis=0, tiled=True)
    hot_int = owners_hot.astype(jnp.int32)
    mine_rank = jnp.cumsum(hot_int, axis=0) - hot_int
    slot_index = jnp.sum(mine_rank * hot_int, axis=1)
    far_index = jnp.where(remote, my_owner * slot_depth + slot_index, 0)
    far_part = jnp.take(
        incoming.reshape(rank_count * slot_depth, block_size, columns), far_index, axis=0
    )
    local_part = jnp.take(own_blocks, my_local, axis=0)
    operand = jnp.where(remote[:, None, None], far_part, local_part).reshape(
        block_rows, slot_count, block_size, columns
    )
    product = jnp.einsum("rsij,rsjk->rik", a_blocks, operand, preferred_element_type=jnp.float32)
    image = product.reshape(block_rows * block_size, columns)
    node_count = rank_count * block_rows * block_size
    gram_local = jnp.einsum("nk,nl->kl", image, image, precision=lax.Precision.HIGHEST)
    gram = lax.psum(gram_local, "rows")
    factor = upper_factor_of(gram / node_count)
    basis_out = jax.scipy.linalg.solve_triangular(factor.T, image.T, lower=True).T
    return (basis_out, factor)


def solution(mesh):
    placed = (
        P(("groups", "rows"), None, None, None),
        P(("groups", "rows"), None),
        P(("groups", "rows"), None),
    )
    return jax.shard_map(
        shards,
        mesh=mesh,
        in_specs=placed,
        out_specs=(P(("groups", "rows"), None), P("groups", None)),
        check_vma=False,
    )
```

profile of v0, /device:TPU:8, one launch (start us, length us, event | category | flops | bytes accessed | tf_op | source)
XLA Modules:
  0.0 299.5 jit_solution(1078787044356833225)
XLA Ops:
  7.2 19.3 %all_gather.3 = s32[128,8]{1,0:T(8,128)S(1)} all-gather(s32[8,8]{1,0:T(8,128)} %param.5), channel_id=1, replica_groups=mesh['groups'=2,'rows'=16] {'rows'}, dimensions={0}, use_global_device_ids=true | all-gather | bytes 4352 | tf_op jit(solution)/shard_map/all_gather | solution.py:22
  26.4 0.1 reshape.362
  26.5 0.1 fusion.33
  26.6 0.2 reduce_window_sum.23
  26.8 0.1 fusion.11
  27.0 2.5 convolution_convert_fusion
  29.5 3.7 %copy.22 = bf16[16,5,256,128]{3,2,1,0:T(8,128)(2,1)} copy(bf16[16,5,256,128]{3,0,2,1:T(8,128)(2,1)S(1)} %convolution_convert_fusion) | data formatting | bytes 10485760 | tf_op jit(solution)/shard_map/convert_element_type | solution.py:45
  33.2 0.0 copy-start.1
  33.3 0.0 copy-start
  33.3 7.7 %all-to-all-start = ((bf16[16,5,256,128]{3,2,1,0:T(8,128)(2,1)}), bf16[16,5,256,128]{3,2,1,0:T(8,128)(2,1)}, u32[]{:S(2)}, u32[]{:S(2)}) async-start(bf16[16,5,256,128]{3,2,1,0:T(8,128)(2,1)} %copy.22), calls=%async_computation | async-start | bytes 10485760 | tf_op jit(solution)/shard_map/all_to_all | solution.py:46
  41.0 0.0 all-reduce.2.cloned.1.call-start
  41.0 0.0 copy-done.1
  41.0 0.1 reshape.361
  41.1 0.1 reshape.365
  41.2 0.1 fusion.23
  41.3 0.1 reduce_window_sum.22
  41.4 0.2 select_reduce_fusion.1
  41.6 0.1 reduce_sum.14
  41.7 0.0 copy-done
  41.7 3.1 %gather_fusion.1 = bf16[64,256,128]{2,1,0:T(8,128)(2,1)} fusion(bf16[8,256,128]{2,1,0:T(8,128)(2,1)S(1)} %bitcast.43, s32[1024]{0:T(1024)S(1)} %pad_clamp_fusion), kind=kCustom, calls=%fused_computation.1 | custom fusion | bytes 8388864 | tf_op jit(solution)/shard_map/jit(_take)/gather | solution.py:54
  44.8 6.4 %copy.24 = bf16[64,256,128]{1,2,0:T(8,128)(2,1)} copy(bf16[64,256,128]{2,1,0:T(8,128)(2,1)} %gather_fusion.1) | data formatting | bytes 8388608 | tf_op jit(solution)/shard_map/jit(_take)/gather | solution.py:54
  51.2 103.1 %all-to-all-done = bf16[16,5,256,128]{3,2,1,0:T(8,128)(2,1)} async-done(((bf16[16,5,256,128]{3,2,1,0:T(8,128)(2,1)}), bf16[16,5,256,128]{3,2,1,0:T(8,128)(2,1)}, u32[]{:S(2)}, u32[]{:S(2)}) %all-to-all-start) | async-done | bytes 5242912 | tf_op jit(solution)/shard_map/all_to_all | solution.py:46
  154.3 5.6 %gather_fusion = bf16[64,256,128]{2,1,0:T(8,128)(2,1)} fusion(bf16[80,256,128]{2,1,0:T(8,128)(2,1)} %bitcast.3, s32[1024]{0:T(1024)S(1)} %pad_clamp_fusion.1), kind=kCustom, calls=%fused_computation | custom fusion | bytes 8388864 | tf_op jit(solution)/shard_map/jit(_take)/gather | solution.py:51
  159.8 6.4 %copy.23 = bf16[8,8,256,128]{2,3,1,0:T(8,128)(2,1)} copy(bf16[8,8,256,128]{3,2,1,0:T(8,128)(2,1)} %bitcast.44) | data formatting | bytes 8388608 | tf_op jit(solution)/shard_map/jit(_take)/gather | solution.py:51
  166.3 8.7 %fusion.8 = f32[8,256,128]{1,2,0:T(8,128)S(1)} fusion(bf16[8,8,256,256]{3,2,1,0:T(8,128)(2,1)} %param.3, bf16[8,8,256,128]{2,3,1,0:T(8,128)(2,1)} %bitcast.45, bf16[8,8,256,128]{2,3,1,0:T(8,128)(2,1)} %copy.23, pred[8,8]{1,0:T(8,128)(4,1)S(1)} %get-tuple-element.17, pred[8,8]{1,0:T(8,128)(4,1)S(1)} %get-tuple-element.18, pred[8,8]{1,0:T(8,128)(4,1)S(1)} %get-tuple-element.16), kind=kOutput, calls=%fused_computation.11 | convolution fusion | flops 1080033280 | bytes 17825984 | tf_op jit(solution)/shard_map/rsij,rsjk->rik/dot_general | solution.py:58
  175.0 1.6 convolution_bitcast_fusion
  176.7 0.0 all-reduce.2.cloned.1.call-update
  176.7 0.3 copy.25
  177.0 88.3 %all-reduce.2.cloned.1.call-done = f32[128,128]{0,1:T(8,128)} async-done(((f32[128,128]{0,1:T(8,128)}), f32[128,128]{0,1:T(8,128)}) %all-reduce.2.cloned.1.call-update) | async-done | bytes 65552 | tf_op jit(solution)/shard_map/psum | solution.py:62
  265.3 0.8 broadcast_multiply_fusion
  266.1 0.1 copy.28
  266.2 0.9 fusion.16
  267.1 11.7 %cholesky.16 = f32[128,128]{1,0:T(8,128)S(1)} custom-call(f32[128,128]{1,0:T(8,128)S(1)} %fusion.16), custom_call_target="Cholesky" | custom-call | tf_op jit(solution)/shard_map/jit(cholesky)/cholesky | solution.py:8
  278.8 0.6 compare_reduce_fusion
  279.5 0.7 fusion.19
  280.1 9.8 %custom-call.7 = f32[1,128,128]{1,2,0:T(8,128)S(1)} custom-call(f32[1,128,128]{2,1,0:T(8,128)S(1)} %get-tuple-element.15), custom_call_target="InvertDiagBlocksLowerTriangular" | custom-call | tf_op jit(solution)/shard_map/jit(_solve_triangular)/triangular_solve | solution.py:64
  289.9 0.7 copy.29
  290.7 1.9 fusion.14
  (9 shorter events, 0.1 us)
Async XLA Ops:
  33.2 7.8 %copy-start.1 = (s32[8,8]{1,0:T(8,128)S(1)}, s32[8,8]{1,0:T(8,128)}, u32[]{:S(2)}) copy-start(s32[8,8]{1,0:T(8,128)} %param.5) | copy-start | bytes 772
  33.3 8.4 %copy-start = (bf16[2048,128]{1,0:T(8,128)(2,1)S(1)}, bf16[2048,128]{1,0:T(8,128)(2,1)}, u32[]{:S(2)}) copy-start(bf16[2048,128]{1,0:T(8,128)(2,1)} %param.4) | copy-start | bytes 1572868
  33.3 121.0 %all-to-all-start = ((bf16[16,5,256,128]{3,2,1,0:T(8,128)(2,1)}), bf16[16,5,256,128]{3,2,1,0:T(8,128)(2,1)}, u32[]{:S(2)}, u32[]{:S(2)}) async-start(bf16[16,5,256,128]{3,2,1,0:T(8,128)(2,1)} %copy.22), calls=%async_computation | async-start | bytes 10485760 | tf_op jit(solution)/shard_map/all_to_all | solution.py:46
  41.0 224.3 %all-reduce.2.cloned.1.call-start = ((), (), s32[]{:S(2)}) async-start(), calls=%async_computation.1 | async-start | bytes 131072 | tf_op jit(solution)/shard_map/psum | solution.py:62
Sparse Core Ops, SparseCore 0:
  176.8 88.4 all-reduce.1
where the time goes:
time: 300 us; the launch traced here: 299 us
  waiting for transfers between devices  191 us (64%)
  local copies, waits for them, and re-layouts  26.6 us (9%)
  other arithmetic  25.3 us (8%)
  blocking collectives  19.3 us (6%)
  matrix products  15 us (5%)
  between operations  14.2 us (5%)
  starting transfers between devices  7.75 us (3%)
    all_to_all x1, waiting for transfers between devices, shards(): lax.all_to_all(outgoing, 'rows', split_axis=0, concat_axis=0, tiled=True)  103 us
    psum x1, waiting for transfers between devices, shards(): gram = lax.psum(gram_local, 'rows')  88.3 us
    all_gather x1, blocking collectives, shards(): lax.all_gather(pattern, 'rows', axis=0, tiled=True)  19.3 us
    another operation x3, other arithmetic, upper_factor_of(): return jnp.linalg.cholesky(matrix).T  12.4 us
    gather x2, local copies, waits for them, and re-layouts, shards(): jnp.take(incoming.reshape(rank_count * slot_depth, block_size, columns),...  12 us
    another operation x1, other arithmetic, shards(): jax.scipy.linalg.solve_triangular(factor.T, image.T, lower=True)  9.81 us
    gather x2, local copies, waits for them, and re-layouts, shards(): local_part = jnp.take(own_blocks, my_local, axis=0)  9.43 us
    dot_general x1, matrix products, shards(): jnp.einsum('rsij,rsjk->rik', a_blocks, operand, preferred_element_type=jn...  8.75 us
  transfers between devices with their start and end apart: 2, of which 2 were waited for; matrix products, arithmetic and copies ran while one was open for 3% of the time, Pallas kernels for 0%

commit v1 on v0

--- a/solution.py
+++ b/solution.py
@@ -2,6 +2,11 @@
 import jax.numpy as jnp
 from jax import lax
 from jax.sharding import PartitionSpec as P
+
+
+def summed_here(block, name):
+    pieces = lax.all_gather(block, name)
+    return jnp.sum(pieces, axis=0)
 
 
 def upper_factor_of(matrix):
@@ -59,7 +64,7 @@
     image = product.reshape(block_rows * block_size, columns)
     node_count = rank_count * block_rows * block_size
     gram_local = jnp.einsum("nk,nl->kl", image, image, precision=lax.Precision.HIGHEST)
-    gram = lax.psum(gram_local, "rows")
+    gram = summed_here(gram_local, "rows")
     factor = upper_factor_of(gram / node_count)
     basis_out = jax.scipy.linalg.solve_triangular(factor.T, image.T, lower=True).T
     return (basis_out, factor)

time: 300 us -> 252 us (0.84)
  waiting for transfers between devices: 191 us -> 141 us
    psum x1 -> x0, waiting for transfers between devices: 88.3 us -> none  [shards(): gram = lax.psum(gram_local, 'rows')]
    all_gather x0 -> x1, waiting for transfers between devices: none -> 38.2 us  [summed_here(): pieces = lax.all_gather(block, name)]
  transfers between devices with their start and end apart: 2 -> 2, of which waited for: 2 -> 2; matrix products, arithmetic and copies ran while one was open for 3% -> 4% of each run, Pallas kernels for 0% -> 0%
where the time goes in v1:
time: 252 us; the launch traced here: 249 us
  waiting for transfers between devices  141 us (56%)
  local copies, waits for them, and re-layouts  26.6 us (11%)
  other arithmetic  24.9 us (10%)
  blocking collectives  19.3 us (8%)
  matrix products  15 us (6%)
  between operations  14.2 us (6%)
  starting transfers between devices  7.75 us (3%)
    all_to_all x1, waiting for transfers between devices, shards(): lax.all_to_all(outgoing, 'rows', split_axis=0, concat_axis=0, tiled=True)  103 us
    all_gather x1, waiting for transfers between devices, summed_here(): pieces = lax.all_gather(block, name)  38.2 us
    all_gather x1, blocking collectives, shards(): lax.all_gather(pattern, 'rows', axis=0, tiled=True)  19.3 us
    another operation x3, other arithmetic, upper_factor_of(): return jnp.linalg.cholesky(matrix).T  12.4 us
    gather x2, local copies, waits for them, and re-layouts, shards(): jnp.take(incoming.reshape(rank_count * slot_depth, block_size, columns),...  12 us
    another operation x1, other arithmetic, shards(): jax.scipy.linalg.solve_triangular(factor.T, image.T, lower=True)  9.81 us
    gather x2, local copies, waits for them, and re-layouts, shards(): local_part = jnp.take(own_blocks, my_local, axis=0)  9.43 us
    dot_general x1, matrix products, shards(): jnp.einsum('rsij,rsjk->rik', a_blocks, operand, preferred_element_type=jn...  8.75 us
  transfers between devices with their start and end apart: 2, of which 2 were waited for; matrix products, arithmetic and copies ran while one was open for 4% of the time, Pallas kernels for 0%

profile of v1, /device:TPU:8, one launch (start us, length us, event | category | flops | bytes accessed | tf_op | source)
XLA Modules:
  0.0 249.0 jit_solution(11759628268833056247)
XLA Ops:
  7.2 19.3 %all_gather.9 = s32[128,8]{1,0:T(8,128)S(1)} all-gather(s32[8,8]{1,0:T(8,128)} %param.5), channel_id=1, replica_groups=mesh['groups'=2,'rows'=16] {'rows'}, dimensions={0}, use_global_device_ids=true | all-gather | bytes 4352 | tf_op jit(solution)/shard_map/all_gather | solution.py:27
  26.4 0.1 reshape.362
  26.5 0.1 fusion.33
  26.6 0.2 reduce_window_sum.23
  26.8 0.1 fusion.11
  27.0 2.5 %convolution_convert_fusion = bf16[16,5,256,128]{3,0,2,1:T(8,128)(2,1)S(1)} fusion(bf16[8,256,128]{2,1,0:T(8,128)(2,1)} %bitcast.43, bf16[16,5,8,1]{2,1,0,3:T(8,128)(2,1)S(1)} %fusion.11), kind=kOutput, calls=%fused_computation.9 | convolution fusion | flops 44564480 | bytes 5768448 | tf_op jit(solution)/shard_map/ekb,bij->ekij/dot_general | solution.py:48
  29.5 3.7 %copy.20 = bf16[16,5,256,128]{3,2,1,0:T(8,128)(2,1)} copy(bf16[16,5,256,128]{3,0,2,1:T(8,128)(2,1)S(1)} %convolution_convert_fusion) | data formatting | bytes 10485760 | tf_op jit(solution)/shard_map/convert_element_type | solution.py:50
  33.2 0.0 copy-start.1
  33.3 0.0 copy-start
  33.3 7.7 %all-to-all-start = ((bf16[16,5,256,128]{3,2,1,0:T(8,128)(2,1)}), bf16[16,5,256,128]{3,2,1,0:T(8,128)(2,1)}, u32[]{:S(2)}, u32[]{:S(2)}) async-start(bf16[16,5,256,128]{3,2,1,0:T(8,128)(2,1)} %copy.20), calls=%async_computation | async-start | bytes 10485760 | tf_op jit(solution)/shard_map/all_to_all | solution.py:51
  41.0 0.0 all-gather.3.cloned.1.call-start
  41.0 0.0 copy-done.1
  41.0 0.1 reshape.361
  41.1 0.1 reshape.365
  41.2 0.1 fusion.23
  41.3 0.1 reduce_window_sum.22
  41.4 0.2 select_reduce_fusion.1
  41.6 0.1 reduce_sum.25
  41.7 0.0 copy-done
  41.7 3.1 %gather_fusion.1 = bf16[64,256,128]{2,1,0:T(8,128)(2,1)} fusion(bf16[8,256,128]{2,1,0:T(8,128)(2,1)S(1)} %bitcast.44, s32[1024]{0:T(1024)S(1)} %pad_clamp_fusion), kind=kCustom, calls=%fused_computation.1 | custom fusion | bytes 8388864 | tf_op jit(solution)/shard_map/jit(_take)/gather | solution.py:59
  44.8 6.4 %copy.22 = bf16[64,256,128]{1,2,0:T(8,128)(2,1)} copy(bf16[64,256,128]{2,1,0:T(8,128)(2,1)} %gather_fusion.1) | data formatting | bytes 8388608 | tf_op jit(solution)/shard_map/jit(_take)/gather | solution.py:59
  51.2 103.1 %all-to-all-done = bf16[16,5,256,128]{3,2,1,0:T(8,128)(2,1)} async-done(((bf16[16,5,256,128]{3,2,1,0:T(8,128)(2,1)}), bf16[16,5,256,128]{3,2,1,0:T(8,128)(2,1)}, u32[]{:S(2)}, u32[]{:S(2)}) %all-to-all-start) | async-done | bytes 5242912 | tf_op jit(solution)/shard_map/all_to_all | solution.py:51
  154.3 5.6 %gather_fusion = bf16[64,256,128]{2,1,0:T(8,128)(2,1)} fusion(bf16[80,256,128]{2,1,0:T(8,128)(2,1)} %bitcast.3, s32[1024]{0:T(1024)S(1)} %pad_clamp_fusion.1), kind=kCustom, calls=%fused_computation | custom fusion | bytes 8388864 | tf_op jit(solution)/shard_map/jit(_take)/gather | solution.py:56
  159.8 6.4 %copy.21 = bf16[8,8,256,128]{2,3,1,0:T(8,128)(2,1)} copy(bf16[8,8,256,128]{3,2,1,0:T(8,128)(2,1)} %bitcast.45) | data formatting | bytes 8388608 | tf_op jit(solution)/shard_map/jit(_take)/gather | solution.py:56
  166.3 8.7 %fusion.8 = f32[8,256,128]{1,2,0:T(8,128)S(1)} fusion(bf16[8,8,256,256]{3,2,1,0:T(8,128)(2,1)} %param.3, bf16[8,8,256,128]{2,3,1,0:T(8,128)(2,1)} %bitcast.46, bf16[8,8,256,128]{2,3,1,0:T(8,128)(2,1)} %copy.21, pred[8,8]{1,0:T(8,128)(4,1)S(1)} %get-tuple-element.17, pred[8,8]{1,0:T(8,128)(4,1)S(1)} %get-tuple-element.18, pred[8,8]{1,0:T(8,128)(4,1)S(1)} %get-tuple-element.16), kind=kOutput, calls=%fused_computation.11 | convolution fusion | flops 1080033280 | bytes 17825984 | tf_op jit(solution)/shard_map/rsij,rsjk->rik/dot_general | solution.py:63
  175.0 1.6 convolution_bitcast_fusion
  176.7 0.0 all-gather.3.cloned.1.call-update
  176.7 0.3 copy.23
  177.0 38.2 %all-gather.3.cloned.1.call-done = f32[2048,128]{1,0:T(8,128)} async-done(((f32[128,128]{1,0:T(8,128)}), f32[2048,128]{1,0:T(8,128)}) %all-gather.3.cloned.1.call-update) | async-done | bytes 1048592 | tf_op jit(solution)/shard_map/all_gather | solution.py:8
  215.2 1.3 reduce_sum.27
  216.5 0.1 copy.25
  216.6 11.7 %cholesky.16 = f32[128,128]{1,0:T(8,128)S(1)} custom-call(f32[128,128]{1,0:T(8,128)S(1)} %fusion.16), custom_call_target="Cholesky" | custom-call | tf_op jit(solution)/shard_map/jit(cholesky)/cholesky | solution.py:13
  228.4 0.6 compare_reduce_fusion
  229.0 0.7 fusion.19
  229.7 9.8 %custom-call.7 = f32[1,128,128]{1,2,0:T(8,128)S(1)} custom-call(f32[1,128,128]{2,1,0:T(8,128)S(1)} %get-tuple-element.15), custom_call_target="InvertDiagBlocksLowerTriangular" | custom-call | tf_op jit(solution)/shard_map/jit(_solve_triangular)/triangular_solve | solution.py:69
  239.5 0.7 copy.26
  240.2 1.9 fusion.14
  (10 shorter events, 0.1 us)
Async XLA Ops:
  33.2 7.8 %copy-start.1 = (s32[8,8]{1,0:T(8,128)S(1)}, s32[8,8]{1,0:T(8,128)}, u32[]{:S(2)}) copy-start(s32[8,8]{1,0:T(8,128)} %param.5) | copy-start | bytes 772
  33.3 8.4 %copy-start = (bf16[2048,128]{1,0:T(8,128)(2,1)S(1)}, bf16[2048,128]{1,0:T(8,128)(2,1)}, u32[]{:S(2)}) copy-start(bf16[2048,128]{1,0:T(8,128)(2,1)} %param.4) | copy-start | bytes 1572868
  33.3 121.0 %all-to-all-start = ((bf16[16,5,256,128]{3,2,1,0:T(8,128)(2,1)}), bf16[16,5,256,128]{3,2,1,0:T(8,128)(2,1)}, u32[]{:S(2)}, u32[]{:S(2)}) async-start(bf16[16,5,256,128]{3,2,1,0:T(8,128)(2,1)} %copy.20), calls=%async_computation | async-start | bytes 10485760 | tf_op jit(solution)/shard_map/all_to_all | solution.py:51
  41.0 174.3 %all-gather.3.cloned.1.call-start = ((), (), s32[]{:S(2)}) async-start(), calls=%async_computation.1 | async-start | bytes 1114112 | tf_op jit(solution)/shard_map/all_gather | solution.py:8
Sparse Core Ops, SparseCore 0:
  176.8 38.3 all-gather.2
